TPU v7x, 128 devices: a whole 4x4x4 slice. The times are simulated.
128 devices in a mesh: ta: 16 (over x_hi, y, core), ha: 8 (over x_lo, z).
Axes of the slice: x: 4 (x_hi: 2, x_lo: 2; x = x_hi * 2 + x_lo), y: 4, z: 4, core: 2. Of those that a mesh axis runs over, the one named last changes fastest.
Arguments:
- activations: bfloat16 [32, 32, 80, 1536], P('ta', 'ha'), may hold values from -6 to 6
- qkv_weight: bfloat16 [1536, 4608], replicated, may hold values from -0.15625 to 0.15625
- out_weight: bfloat16 [1536, 1536], replicated, may hold values from -0.15625 to 0.15625
- query_gain: float32 [128], replicated, may hold values from 0.8 to 2.5
- key_gain: float32 [128], replicated, may hold values from 0.8 to 2.5
- clip_lengths: int32 [4], replicated, may hold values from 1 to 16, 32 in all
- extents: int32 [16, 8, 2], replicated, may hold values from 0 to 1
Outputs:
- mixed: bfloat16 [32, 32, 80, 1536], P('ta', 'ha')
Inputs may be any that keep to these rules, and one draw needn't show every extreme that they name: `extents`: each is a reach of 0 or 1 tiles. `clip_lengths`: the 4 lengths sum to 32.
All inputs are finite; a program needn't handle non-finite values.
Results may differ from a plain program's by a relative error of at most 0.011.
Values may be sent and summed in bfloat16 or wider, within the bound.
No kernel may reach another device: no remote copies, remote signals or barrier semaphores. Data moves between devices by JAX's collectives and lax.ppermute only.
A program may use at most 256 MiB of HBM per device.

v0:
```python
import functools
import math

import jax
import jax.numpy as jnp
from jax import lax
from jax.experimental import pallas as pl
from jax.experimental.pallas import tpu as pltpu
from jax.sharding import PartitionSpec as P

norm_eps = 1e-06
f32 = jnp.float32
bf16 = jnp.bfloat16
hd = 128
group = 4
cost = 2.5
vmem_bytes = 60 << 20


def normed(features, gain):
    mean_sq = jnp.mean(features * features, axis=-1, keepdims=True)
    return (features * lax.rsqrt(mean_sq + norm_eps) * gain).astype(bf16)


def same_clip(first, second, lengths):
    end = 0
    same = None
    for c in range(lengths.shape[0] - 1):
        end = end + lengths[c]
        here = (first >= end) == (second >= end)
        same = here if same is None else same & here
    return same


def core_partner(t):
    return t + 1 - 2 * lax.rem(t, 2)


def y_partner(t):
    return t - 1 + 2 * lax.rem(t, 2)


def itself(t):
    return t


def reach_flags(query_of, key_of, extents, lengths):
    t, h = lax.axis_index("ta"), lax.axis_index("ha")
    count = lax.axis_size("ta")
    query, key = query_of(t), key_of(t)
    inside = (query >= 0) & (query < count) & (key >= 0) & (key < count)
    safe = jnp.clip(query, 0, count - 1)
    near = inside & (jnp.abs(query - key) <= extents[safe, h, 0])
    pairs = [[near & same_clip(2 * safe + i, 2 * key + j, lengths) for j in range(2)] for i in range(2)]
    return pairs, extents[safe, h, 1] >= 1


def any_of(pairs):
    return pairs[0][0] | pairs[0][1] | pairs[1][0] | pairs[1][1]


def home_pieces():
    return [(0, True), (1, True)]


def near_pieces(frames):
    h = lax.axis_index("ha")
    sides = [h > 0, h < lax.axis_size("ha") - 1]
    return [(frame, side) for frame in frames for side in sides]


def column_masks(pairs, half, pieces):
    where = lax.broadcasted_iota(jnp.int32, (1, half * len(pieces)), 1)
    masks = []
    for i in range(2):
        row = None
        for a, (frame, valid) in enumerate(pieces):
            on = (pairs[i][frame] & valid).astype(f32)
            part = jnp.where((where >= a * half) & (where < (a + 1) * half), on, 0.0)
            row = part if row is None else row + part
        masks.append(row)
    return masks


def attend(q, k, v, mask):
    scores = lax.dot_general(q, k, (((1,), (1,)), ((), ())), preferred_element_type=f32)
    weights = (jnp.exp2(scores * (math.log2(math.e) / math.sqrt(hd))) * mask).astype(bf16)
    wide = jnp.concatenate([v, jnp.ones_like(v)], axis=1)
    return jnp.dot(weights, wide, preferred_element_type=f32)


def attend_group(q_ref, kv_refs, pairs, pieces, sink):
    half = q_ref.shape[0] // 2
    masks = column_masks(pairs, half, pieces)
    for b in range(q_ref.shape[1] // hd):
        lanes = slice(b * hd, (b + 1) * hd)
        k = jnp.concatenate([ref[0, :, lanes] for ref in kv_refs], axis=0)
        v = jnp.concatenate([ref[1, :, lanes] for ref in kv_refs], axis=0)
        for i in range(2):
            rows = slice(i * half, (i + 1) * half)
            out = attend(q_ref[rows, lanes], k, v, masks[i])
            sink(b, rows, lanes, out[:, :hd], out[:, hd:])


def lane_id():
    return lax.broadcasted_iota(jnp.int32, (1, hd), 1)


def project_kernel(x_ref, w_ref, gain_ref, q_ref):
    out = jnp.dot(x_ref[...], w_ref[...], preferred_element_type=f32)
    for b in range(out.shape[1] // hd):
        lanes = slice(b * hd, (b + 1) * hd)
        q_ref[:, lanes] = normed(out[:, lanes], gain_ref[...])


def keys_values(x_refs, wk_ref, wv_ref, gain_ref, kv_ref):
    first = 0
    for x_ref in x_refs:
        rows = slice(first, first + x_ref.shape[0])
        first = rows.stop
        out = jnp.dot(x_ref[...], wk_ref[...], preferred_element_type=f32)
        for b in range(out.shape[1] // hd):
            lanes = slice(b * hd, (b + 1) * hd)
            kv_ref[0, rows, lanes] = normed(out[:, lanes], gain_ref[...])
        kv_ref[1, rows, :] = jnp.dot(x_ref[...], wv_ref[...], preferred_element_type=f32).astype(bf16)


def add_total(s_ref, head, rows, total):
    here = (lane_id() & (hd // 2 - 1)) == head
    s_ref[rows, :] = jnp.where(here, s_ref[rows, :] + total, s_ref[rows, :])


def begin(s_ref, t_ref):
    @pl.when(pl.program_id(0) == 0)
    def _():
        s_ref[...] = jnp.zeros_like(s_ref) if t_ref is None else t_ref[...]


def gather(q_ref, a_ref, o_ref, s_ref, choices):
    step = pl.program_id(0)
    taken = None
    for condition, kv_refs, pairs, pieces in choices:
        taken = condition if taken is None else taken | condition

        def run(kv_refs=kv_refs, pairs=pairs, pieces=pieces):
            def sink(b, rows, lanes, out, total):
                o_ref[rows, lanes] = out if a_ref is None else a_ref[rows, lanes] + out
                add_total(s_ref, step * group + b, rows, total)

            attend_group(q_ref, kv_refs, pairs, pieces, sink)

        pl.when(condition)(run)

    @pl.when(jnp.logical_not(taken))
    def _():
        o_ref[...] = jnp.zeros_like(o_ref) if a_ref is None else a_ref[...]


def near_needed(ext, lens):
    needed = None
    for query_of in (itself, core_partner, y_partner):
        pairs, reach = reach_flags(query_of, itself, ext, lens)
        need = any_of(pairs) & reach
        needed = need if needed is None else needed | need
    return needed


def home_kernel(ext, lens, q_ref, x_ref, wk_ref, wv_ref, gain_ref, o_ref, s_ref, kv_ref, late_ref):
    step = pl.program_id(0)
    begin(s_ref, None)
    keys_values([x_ref], wk_ref, wv_ref, gain_ref, kv_ref)
    pairs, _ = reach_flags(itself, itself, ext, lens)
    gather(q_ref, None, o_ref, s_ref, [(any_of(pairs), [kv_ref], pairs, home_pieces())])

    @pl.when(step == 0)
    def _():
        late_ref[...] = x_ref[x_ref.shape[0] // 2 :, :]


def first_kernel(ext, lens, xu, xd, wk_ref, wv_ref, gain_ref, near_ref):
    @pl.when(near_needed(ext, lens))
    def _():
        keys_values([xu, xd], wk_ref, wv_ref, gain_ref, near_ref)


def y_kernel(ext, lens, q_ref, kv_ref, near_ref, o_ref, s_ref):
    begin(s_ref, None)
    pairs, reach = reach_flags(y_partner, itself, ext, lens)
    active = any_of(pairs)
    gather(
        q_ref,
        None,
        o_ref,
        s_ref,
        [
            (active & reach, [kv_ref, near_ref], pairs, home_pieces() + near_pieces([0])),
            (active & jnp.logical_not(reach), [kv_ref], pairs, home_pieces()),
        ],
    )


def second_kernel(
    ext, lens, xu, xd, wk_ref, wv_ref, gain_ref, q_ref, a_ref, t_ref, o_ref, near_ref, s_ref, part
):
    step = pl.program_id(0)
    begin(s_ref, t_ref)

    @pl.when(near_needed(ext, lens))
    def _():
        keys_values([xu, xd], wk_ref, wv_ref, gain_ref, near_ref)

    pairs, reach = reach_flags(y_partner, itself, ext, lens)
    gather(q_ref, a_ref, part, s_ref, [(any_of(pairs) & reach, [near_ref], pairs, near_pieces([1]))])
    width = part.shape[1]
    o_ref[:, pl.ds(pl.multiple_of(step * width, width), width)] = part[...].astype(bf16)

    @pl.when(step == pl.num_programs(0) - 1)
    def _():
        high = s_ref[...].astype(bf16)
        low = (s_ref[...] - high.astype(f32)).astype(bf16)
        o_ref[:, o_ref.shape[1] - hd :] = jnp.where(lane_id() < hd // 2, high, low)


def near_kernel(ext, lens, q_ref, a_ref, t_ref, first_ref, last_ref, o_ref, s_ref):
    begin(s_ref, t_ref)
    pairs, reach = reach_flags(itself, itself, ext, lens)
    keys = [first_ref, last_ref]
    gather(q_ref, a_ref, o_ref, s_ref, [(any_of(pairs) & reach, keys, pairs, near_pieces([0, 1]))])


def core_kernel(ext, lens, q_ref, a_ref, t_ref, home_ref, first_ref, last_ref, o_ref, s_ref):
    begin(s_ref, t_ref)
    pairs, reach = reach_flags(itself, core_partner, ext, lens)
    active = any_of(pairs)
    gather(
        q_ref,
        a_ref,
        o_ref,
        s_ref,
        [
            (active & reach, [home_ref, first_ref, last_ref], pairs, home_pieces() + near_pieces([0, 1])),
            (active & jnp.logical_not(reach), [home_ref], pairs, home_pieces()),
        ],
    )


def close_kernel(a_ref, t_ref, y_ref, w_ref, out_ref, mixed):
    width = a_ref.shape[1]
    back = y_ref[:, width:].astype(f32)
    for b in range(width // hd):
        lanes = slice(b * hd, (b + 1) * hd)
        low = hd // 2 + b
        total = t_ref[:, b : b + 1] + (back[:, b : b + 1] + back[:, low : low + 1])
        value = a_ref[:, lanes] + y_ref[:, lanes].astype(f32)
        mixed[:, lanes] = (value / total).astype(bf16)
    out_ref[...] = jnp.dot(mixed[...], w_ref[...], preferred_element_type=f32).astype(bf16)


def whole(shape):
    return pl.BlockSpec(shape, lambda g: (0,) * len(shape))


def by_group(rows):
    return pl.BlockSpec((rows, group * hd), lambda g: (0, g))


def call(kernel, steps, ins, outs, flops, scratch=(), after=None):
    run, specs, arrays = kernel, [spec for _, spec in ins], [array for array, _ in ins]
    if after is not None:
        place = len(ins)
        specs, arrays = specs + [pl.BlockSpec(memory_space=pl.ANY)], arrays + [after]

        def run(*refs):
            kernel(*refs[:place], *refs[place + 1 :])

    return pl.pallas_call(
        run,
        grid=(steps,),
        in_specs=specs,
        out_specs=[spec for spec, _, _ in outs],
        out_shape=[jax.ShapeDtypeStruct(shape, dtype) for _, shape, dtype in outs],
        scratch_shapes=list(scratch),
        compiler_params=pltpu.CompilerParams(vmem_limit_bytes=vmem_bytes),
        cost_estimate=pl.CostEstimate(flops=int(flops), bytes_accessed=1, transcendentals=0),
    )(*arrays)


def body(activations, qkv_weight, out_weight, query_gain, key_gain, clip_lengths, extents):
    frames, rows, cols, model = activations.shape
    half = rows * cols
    tile = frames * half
    inner = out_weight.shape[0]
    steps = inner // (group * hd)
    x = activations.reshape(tile, model)
    q_gain, k_gain = query_gain.reshape(1, hd), key_gain.reshape(1, hd)
    height, time = lax.axis_size("ha"), lax.axis_size("ta")
    smem = pl.BlockSpec(memory_space=pltpu.SMEM)

    def to_heights(a):
        return (
            lax.ppermute(a, "ha", [(i, i + 1) for i in range(height - 1)]),
            lax.ppermute(a, "ha", [(i + 1, i) for i in range(height - 1)]),
        )

    def to_core(a):
        return lax.ppermute(a, "ta", [(i, i ^ 1) for i in range(time)])

    def to_y(a):
        route = [(i, i + 1) for i in range(1, time - 1, 2)]
        return lax.ppermute(a, "ta", route + [(b, a) for a, b in route])

    def w_of(part):
        return (qkv_weight, pl.BlockSpec((model, group * hd), lambda g: (0, part * steps + g)))

    unit = cost * 2.0 * tile * tile * inner
    mat = cost * 2.0 * tile * model * inner
    total_spec = whole((tile, hd))
    sums = [(by_group(tile), (tile, inner), f32), (total_spec, (tile, hd), f32)]
    kv_spec = pl.BlockSpec((2, tile, group * hd), lambda g: (0, 0, g))
    kv_out = (kv_spec, (2, tile, inner), bf16)
    flags = [(extents, smem), (clip_lengths, smem)]
    kv_weights = [w_of(1), w_of(2), (k_gain, whole((1, hd)))]

    up_first, down_first = to_heights(activations[0].reshape(half, model))
    (q,) = call(
        project_kernel,
        steps,
        [(x, whole((tile, model))), w_of(0), (q_gain, whole((1, hd)))],
        [(by_group(tile), (tile, inner), bf16)],
        mat,
    )
    q_y = to_y(q)
    own, own_total, kv_home, late = call(
        home_kernel,
        steps,
        flags + [(q, by_group(tile)), (x, whole((tile, model)))] + kv_weights,
        sums + [kv_out, (whole((half, model)), (half, model), bf16)],
        unit + 2 * mat,
    )
    up_last, down_last = to_heights(late)
    kv_core = to_core(kv_home)

    def partial(acc, total):
        return [(acc, by_group(tile)), (total, total_spec)]

    def neighbours(up, down):
        return [(up, whole((half, model))), (down, whole((half, model)))]

    (near_first,) = call(
        first_kernel,
        steps,
        flags + neighbours(up_first, down_first) + kv_weights,
        [kv_out],
        2 * mat,
        after=own_total,
    )
    near_first_core = to_core(near_first)
    y, y_total = call(
        y_kernel,
        steps,
        flags + [(q_y, by_group(tile)), (kv_home, kv_spec), (near_first, kv_spec)],
        sums,
        2 * unit,
    )
    wide = (tile, inner + hd)
    y_part, near_last = call(
        second_kernel,
        steps,
        flags + neighbours(up_last, down_last) + kv_weights + [(q_y, by_group(tile))] + partial(y, y_total),
        [(whole(wide), wide, bf16), kv_out],
        unit + 2 * mat,
        [pltpu.VMEM((tile, hd), f32), pltpu.VMEM((tile, group * hd), f32)],
    )
    y_back = to_y(y_part)
    near_last_core = to_core(near_last)

    own, own_total = call(
        near_kernel,
        steps,
        flags + [(q, by_group(tile))] + partial(own, own_total) + [(near_first, kv_spec), (near_last, kv_spec)],
        sums,
        2 * unit,
    )
    own, own_total = call(
        core_kernel,
        steps,
        flags
        + [(q, by_group(tile))]
        + partial(own, own_total)
        + [(kv, kv_spec) for kv in (kv_core, near_first_core, near_last_core)],
        sums,
        3 * unit,
    )
    cut = tile // 4
    (result,) = call(
        close_kernel,
        4,
        [(a, pl.BlockSpec((cut, a.shape[1]), lambda g: (g, 0))) for a in (own, own_total, y_back)]
        + [(out_weight, whole((inner, model)))],
        [(pl.BlockSpec((cut, model), lambda g: (g, 0)), (tile, model), bf16)],
        mat,
        [pltpu.VMEM((cut, inner), bf16)],
    )
    return result.reshape(frames, rows, cols, model)


def solution(mesh):
    placed = (P("ta", "ha", None, None), P(), P(), P(), P(), P(), P())
    return jax.shard_map(
        body, mesh=mesh, in_specs=placed, out_specs=P("ta", "ha", None, None), check_vma=False
    )
```

profile of v0, /device:TPU:49, one launch (start us, length us, event | category | flops | bytes accessed | tf_op | source)
XLA Modules:
  0.0 143.1 jit_solution(9590373815140845844)
XLA Ops:
  0.0 1.3 slice.3
  1.3 3.5 %collective-permute-start = (bf16[320,1536]{1,0:T(8,128)(2,1)S(1)}, bf16[320,1536]{1,0:T(8,128)(2,1)S(1)}, u32[]{:S(2)}, u32[]{:S(2)}) collective-permute-start(bf16[320,1536]{1,0:T(8,128)(2,1)S(1)} %bitcast.5), channel_id=1, source_target_pairs={{0,1},{1,2},{2,3},{3,4},{4,5},{5,6},{6,7},{8,9},{9,10},{10,11},{11... | collective-permute-start | bytes 2949128 | tf_op jit(solution)/shard_map/ppermute | solution.py:301
  4.8 1.9 %collective-permute-start.1 = (bf16[320,1536]{1,0:T(8,128)(2,1)S(1)}, bf16[320,1536]{1,0:T(8,128)(2,1)S(1)}, u32[]{:S(2)}, u32[]{:S(2)}) collective-permute-start(bf16[320,1536]{1,0:T(8,128)(2,1)S(1)} %bitcast.6), channel_id=1, source_target_pairs={{1,0},{2,1},{3,2},{4,3},{5,4},{6,5},{7,6},{9,8},{10,9},{11,10},{12... | collective-permute-start | bytes 2949128 | tf_op jit(solution)/shard_map/ppermute | solution.py:302
  6.8 0.0 copy-start
  6.8 7.4 %shard_map.73.q_ref = bf16[640,1536]{1,0:T(8,128)(2,1)} custom-call(bf16[640,1536]{1,0:T(8,128)(2,1)} %bitcast.7, bf16[1536,4608]{1,0:T(8,128)(2,1)} %wv_ref.3, f32[1,128]{1,0:T(1,128)} %bitcast.9), custom_call_target="tpu_custom_call" | custom-call | flops 7549747200 | bytes 1 | tf_op jit(solution)/shard_map/pallas_call | solution.py:276
  14.2 3.9 %collective-permute-start.4 = (bf16[640,1536]{1,0:T(8,128)(2,1)}, bf16[640,1536]{1,0:T(8,128)(2,1)}, u32[]{:S(2)}, u32[]{:S(2)}) collective-permute-start(bf16[640,1536]{1,0:T(8,128)(2,1)} %shard_map.73.q_ref), channel_id=1, source_target_pairs={{8,16},{24,32},{40,48},{56,64},{72,80},{88,96},{104,112},{16,8},{3... | collective-permute-start | bytes 5898248 | tf_op jit(solution)/shard_map/ppermute | solution.py:310
  18.1 0.0 copy-done
  18.1 0.7 copy.13.ext.refs_0_
  18.9 18.2 %shard_map.74 = (f32[640,1536]{1,0:T(8,128)}, f32[640,128]{1,0:T(8,128)}, bf16[2,640,1536]{2,1,0:T(8,128)(2,1)}, bf16[320,1536]{1,0:T(8,128)(2,1)}) custom-call(s32[16,8,2]{2,1,0:T(8,128)} %copy.13.ext.refs_0_, s32[4]{0:T(128)} %lens.9, bf16[640,1536]{1,0:T(8,128)(2,1)} %shard_map.73.q_ref, bf16[640,1536]{1,0:T(8,128)(2,1)} %bitcast.8, ...), custom_call_target="tpu_custom_call" | custom-call | flops 18245222400 | bytes 1 | tf_op jit(solution)/shard_map/pallas_call | solution.py:276
  37.0 3.5 %collective-permute-start.2 = (bf16[320,1536]{1,0:T(8,128)(2,1)}, bf16[320,1536]{1,0:T(8,128)(2,1)}, u32[]{:S(2)}, u32[]{:S(2)}) collective-permute-start(bf16[320,1536]{1,0:T(8,128)(2,1)} %get-tuple-element.19), channel_id=1, source_target_pairs={{0,1},{1,2},{2,3},{3,4},{4,5},{5,6},{6,7},{8,9},{9,10},{10,11},{11... | collective-permute-start | bytes 2949128 | tf_op jit(solution)/shard_map/ppermute | solution.py:301
  40.5 2.8 %collective-permute-start.3 = (bf16[320,1536]{1,0:T(8,128)(2,1)}, bf16[320,1536]{1,0:T(8,128)(2,1)}, u32[]{:S(2)}, u32[]{:S(2)}) collective-permute-start(bf16[320,1536]{1,0:T(8,128)(2,1)} %get-tuple-element.19), channel_id=1, source_target_pairs={{1,0},{2,1},{3,2},{4,3},{5,4},{6,5},{7,6},{9,8},{10,9},{11,10},{12... | collective-permute-start | bytes 2949128 | tf_op jit(solution)/shard_map/ppermute | solution.py:302
  43.3 0.0 collective-permute-done.refs_2_
  43.3 0.0 copy-start.2
  43.3 0.1 collective-permute-start.5
  43.4 0.0 collective-permute-done.1.refs_3_
  43.4 0.0 copy-start.3
  43.4 0.8 copy-done.2
  44.3 0.4 copy-done.3
  44.6 11.0 %shard_map.75.near_ref.first_ref = bf16[2,640,1536]{2,1,0:T(8,128)(2,1)} custom-call(s32[16,8,2]{2,1,0:T(8,128)} %copy.13.ext.refs_0_, s32[4]{0:T(128)} %lens.9, bf16[320,1536]{1,0:T(8,128)(2,1)} %copy-done.2, bf16[320,1536]{1,0:T(8,128)(2,1)} %copy-done.3, bf16[1536,4608]{1,0:T(8,128)(2,1)} %wv_ref.3, bf16[1536,4608]{1,0:T(8,128)(2,1)} %wv_ref.3, ...), custom_call_target="tpu_custom_call" | custom-call | flops 15099494400 | bytes 1 | tf_op jit(solution)/shard_map/pallas_call | solution.py:276
  55.6 0.3 collective-permute-start.6
  55.9 0.0 collective-permute-done.4.q_ref
  55.9 9.9 %shard_map.76 = (f32[640,1536]{1,0:T(8,128)}, f32[640,128]{1,0:T(8,128)}) custom-call(s32[16,8,2]{2,1,0:T(8,128)} %copy.13.ext.refs_0_, s32[4]{0:T(128)} %lens.9, bf16[640,1536]{1,0:T(8,128)(2,1)} %collective-permute-done.4.q_ref, bf16[2,640,1536]{2,1,0:T(8,128)(2,1)} %get-tuple-element.20.kv_ref, bf16[2,640,1536]{2,1,0:T(8,128)(2,1)} %shard_map.75.near_ref.first_ref), custom_call_target="tpu_custom_call" | custom-call | flops 6291456000 | bytes 1 | tf_op jit(solution)/shard_map/pallas_call | solution.py:276
  65.8 0.0 collective-permute-done.2.xu
  65.8 0.4 collective-permute-done.3.xd
  66.2 13.8 %shard_map.77 = (bf16[640,1664]{1,0:T(8,128)(2,1)}, bf16[2,640,1536]{2,1,0:T(8,128)(2,1)}) custom-call(s32[16,8,2]{2,1,0:T(8,128)} %copy.13.ext.refs_0_, s32[4]{0:T(128)} %lens.9, bf16[320,1536]{1,0:T(8,128)(2,1)} %collective-permute-done.2.xu, bf16[320,1536]{1,0:T(8,128)(2,1)} %collective-permute-done.3.xd, bf16[1536,4608]{1,0:T(8,128)(2,1)} %wv_ref.3, ...), custom_call_target="tpu_custom_call" | custom-call | flops 18245222400 | bytes 1 | tf_op jit(solution)/shard_map/pallas_call | solution.py:276
  80.0 0.4 collective-permute-start.7
  80.4 14.1 %collective-permute-start.8 = (bf16[640,1664]{1,0:T(8,128)(2,1)}, bf16[640,1664]{1,0:T(8,128)(2,1)}, u32[]{:S(2)}, u32[]{:S(2)}) collective-permute-start(bf16[640,1664]{1,0:T(8,128)(2,1)} %get-tuple-element.28), channel_id=1, source_target_pairs={{8,16},{24,32},{40,48},{56,64},{72,80},{88,96},{104,112},{16,8},{3... | collective-permute-start | bytes 6389768 | tf_op jit(solution)/shard_map/ppermute | solution.py:310
  94.6 15.5 %shard_map.78 = (f32[640,1536]{1,0:T(8,128)}, f32[640,128]{1,0:T(8,128)}) custom-call(s32[16,8,2]{2,1,0:T(8,128)} %copy.13.ext.refs_0_, s32[4]{0:T(128)} %lens.9, bf16[640,1536]{1,0:T(8,128)(2,1)} %shard_map.73.q_ref, f32[640,1536]{1,0:T(8,128)} %get-tuple-element.17.a_ref, f32[640,128]{1,0:T(8,128)} %get-tuple-element.18.refs_7_.t_ref, ...), custom_call_target="tpu_custom_call" | custom-call | flops 6291456000 | bytes 1 | tf_op jit(solution)/shard_map/pallas_call | solution.py:276
  110.0 0.0 collective-permute-done.5.home_ref
  110.0 0.0 collective-permute-done.6.first_ref
  110.1 0.0 copy-start.1
  110.1 0.0 collective-permute-done.7.last_ref
  110.1 1.9 %copy-done.1 = bf16[2,640,1536]{2,1,0:T(8,128)(2,1)} copy-done((bf16[2,640,1536]{2,1,0:T(8,128)(2,1)}, bf16[2,640,1536]{2,1,0:T(8,128)(2,1)S(1)}, u32[]{:S(2)}) %copy-start.1) | copy-done | bytes 3932184
  112.0 21.9 %shard_map.79 = (f32[640,1536]{1,0:T(8,128)}, f32[640,128]{1,0:T(8,128)}) custom-call(s32[16,8,2]{2,1,0:T(8,128)} %copy.13.ext.refs_0_, s32[4]{0:T(128)} %lens.9, bf16[640,1536]{1,0:T(8,128)(2,1)} %shard_map.73.q_ref, f32[640,1536]{1,0:T(8,128)} %get-tuple-element.24.a_ref, f32[640,128]{1,0:T(8,128)} %get-tuple-element.25.t_ref, ...), custom_call_target="tpu_custom_call" | custom-call | flops 9437184000 | bytes 1 | tf_op jit(solution)/shard_map/pallas_call | solution.py:276
  133.9 0.0 collective-permute-done.8.y_ref
  133.9 9.2 %shard_map.80 = bf16[640,1536]{1,0:T(8,128)(2,1)} custom-call(f32[640,1536]{1,0:T(8,128)} %get-tuple-element.26.a_ref, f32[640,128]{1,0:T(8,128)} %get-tuple-element.27.t_ref, bf16[640,1664]{1,0:T(8,128)(2,1)} %collective-permute-done.8.y_ref, bf16[1536,1536]{1,0:T(8,128)(2,1)} %w_ref.3), custom_call_target="tpu_custom_call" | custom-call | flops 7549747200 | bytes 1 | tf_op jit(solution)/shard_map/pallas_call | solution.py:276
Async XLA Ops:
  1.3 42.0 %collective-permute-start = (bf16[320,1536]{1,0:T(8,128)(2,1)S(1)}, bf16[320,1536]{1,0:T(8,128)(2,1)S(1)}, u32[]{:S(2)}, u32[]{:S(2)}) collective-permute-start(bf16[320,1536]{1,0:T(8,128)(2,1)S(1)} %bitcast.5), channel_id=1, source_target_pairs={{0,1},{1,2},{2,3},{3,4},{4,5},{5,6},{6,7},{8,9},{9,10},{10,11},{11... | collective-permute-start | bytes 2949128 | tf_op jit(solution)/shard_map/ppermute | solution.py:301
  4.8 38.6 %collective-permute-start.1 = (bf16[320,1536]{1,0:T(8,128)(2,1)S(1)}, bf16[320,1536]{1,0:T(8,128)(2,1)S(1)}, u32[]{:S(2)}, u32[]{:S(2)}) collective-permute-start(bf16[320,1536]{1,0:T(8,128)(2,1)S(1)} %bitcast.6), channel_id=1, source_target_pairs={{1,0},{2,1},{3,2},{4,3},{5,4},{6,5},{7,6},{9,8},{10,9},{11,10},{12... | collective-permute-start | bytes 2949128 | tf_op jit(solution)/shard_map/ppermute | solution.py:302
  6.8 11.4 %copy-start = (s32[16,8,2]{0,2,1:T(2,128)S(1)}, s32[16,8,2]{0,2,1:T(2,128)}, u32[]{:S(2)}) copy-start(s32[16,8,2]{0,2,1:T(2,128)} %param.13) | copy-start | bytes 3076
  14.2 41.7 %collective-permute-start.4 = (bf16[640,1536]{1,0:T(8,128)(2,1)}, bf16[640,1536]{1,0:T(8,128)(2,1)}, u32[]{:S(2)}, u32[]{:S(2)}) collective-permute-start(bf16[640,1536]{1,0:T(8,128)(2,1)} %shard_map.73.q_ref), channel_id=1, source_target_pairs={{8,16},{24,32},{40,48},{56,64},{72,80},{88,96},{104,112},{16,8},{3... | collective-permute-start | bytes 5898248 | tf_op jit(solution)/shard_map/ppermute | solution.py:310
  37.0 28.8 %collective-permute-start.2 = (bf16[320,1536]{1,0:T(8,128)(2,1)}, bf16[320,1536]{1,0:T(8,128)(2,1)}, u32[]{:S(2)}, u32[]{:S(2)}) collective-permute-start(bf16[320,1536]{1,0:T(8,128)(2,1)} %get-tuple-element.19), channel_id=1, source_target_pairs={{0,1},{1,2},{2,3},{3,4},{4,5},{5,6},{6,7},{8,9},{9,10},{10,11},{11... | collective-permute-start | bytes 2949128 | tf_op jit(solution)/shard_map/ppermute | solution.py:301
  40.5 25.7 %collective-permute-start.3 = (bf16[320,1536]{1,0:T(8,128)(2,1)}, bf16[320,1536]{1,0:T(8,128)(2,1)}, u32[]{:S(2)}, u32[]{:S(2)}) collective-permute-start(bf16[320,1536]{1,0:T(8,128)(2,1)} %get-tuple-element.19), channel_id=1, source_target_pairs={{1,0},{2,1},{3,2},{4,3},{5,4},{6,5},{7,6},{9,8},{10,9},{11,10},{12... | collective-permute-start | bytes 2949128 | tf_op jit(solution)/shard_map/ppermute | solution.py:302
  43.3 0.9 copy-start.2
  43.3 66.7 %collective-permute-start.5 = (bf16[2,640,1536]{2,1,0:T(8,128)(2,1)}, bf16[2,640,1536]{2,1,0:T(8,128)(2,1)}, u32[]{:S(2)}, u32[]{:S(2)}) collective-permute-start(bf16[2,640,1536]{2,1,0:T(8,128)(2,1)} %get-tuple-element.20.kv_ref), channel_id=1, source_target_pairs={{0,8},{8,0},{16,24},{24,16},{32,40},{40,32},{48,56},{56,48},{64,72... | collective-permute-start | bytes 11796488 | tf_op jit(solution)/shard_map/ppermute | solution.py:306
  43.4 1.2 copy-start.3
  55.6 54.4 %collective-permute-start.6 = (bf16[2,640,1536]{2,1,0:T(8,128)(2,1)}, bf16[2,640,1536]{2,1,0:T(8,128)(2,1)S(1)}, u32[]{:S(2)}, u32[]{:S(2)}) collective-permute-start(bf16[2,640,1536]{2,1,0:T(8,128)(2,1)} %shard_map.75.near_ref.first_ref), channel_id=1, source_target_pairs={{0,8},{8,0},{16,24},{24,16},{32,40},{40,32},{48,56},{56,48},{64,72... | collective-permute-start | bytes 11796488 | tf_op jit(solution)/shard_map/ppermute | solution.py:306
  80.0 30.1 %collective-permute-start.7 = (bf16[2,640,1536]{2,1,0:T(8,128)(2,1)}, bf16[2,640,1536]{2,1,0:T(8,128)(2,1)}, u32[]{:S(2)}, u32[]{:S(2)}) collective-permute-start(bf16[2,640,1536]{2,1,0:T(8,128)(2,1)} %get-tuple-element.23.last_ref), channel_id=1, source_target_pairs={{0,8},{8,0},{16,24},{24,16},{32,40},{40,32},{48,56},{56,48},{64,72... | collective-permute-start | bytes 11796488 | tf_op jit(solution)/shard_map/ppermute | solution.py:306
  80.4 53.5 %collective-permute-start.8 = (bf16[640,1664]{1,0:T(8,128)(2,1)}, bf16[640,1664]{1,0:T(8,128)(2,1)}, u32[]{:S(2)}, u32[]{:S(2)}) collective-permute-start(bf16[640,1664]{1,0:T(8,128)(2,1)} %get-tuple-element.28), channel_id=1, source_target_pairs={{8,16},{24,32},{40,48},{56,64},{72,80},{88,96},{104,112},{16,8},{3... | collective-permute-start | bytes 6389768 | tf_op jit(solution)/shard_map/ppermute | solution.py:310
  110.1 2.0 %copy-start.1 = (bf16[2,640,1536]{2,1,0:T(8,128)(2,1)}, bf16[2,640,1536]{2,1,0:T(8,128)(2,1)S(1)}, u32[]{:S(2)}) copy-start(bf16[2,640,1536]{2,1,0:T(8,128)(2,1)S(1)} %collective-permute-done.6.first_ref) | copy-start | bytes 11796484
where the time goes:
time: 145 us; the launch traced here: 143 us
  Pallas kernels  107 us (74%)
  starting transfers between devices  30.5 us (21%)
  local copies, waits for them, and re-layouts  5.13 us (4%)
    pallas_call x8, Pallas kernels, call(): pl.pallas_call(run, grid=(steps,), in_specs=specs, out_specs=[spec for sp...  107 us
    ppermute x2, starting transfers between devices, to_y(): return lax.ppermute(a, 'ta', route + [(b, a) for a, b in route])  18 us
    ppermute x2, starting transfers between devices, to_heights(): lax.ppermute(a, 'ha', [(i, i + 1) for i in range(height - 1)])  7.03 us
    ppermute x2, starting transfers between devices, to_heights(): lax.ppermute(a, 'ha', [(i + 1, i) for i in range(height - 1)])  4.68 us
    unnamed x9, local copies, waits for them, and re-layouts  3.86 us
  transfers between devices with their start and end apart: 9, of which 1 were waited for; matrix products, arithmetic and copies ran while one was open for 1% of the time, Pallas kernels for 68%

commit v1 on v0

--- a/solution.py
+++ b/solution.py
@@ -65,8 +65,7 @@
 
 def near_pieces(frames):
     h = lax.axis_index("ha")
-    sides = [h > 0, h < lax.axis_size("ha") - 1]
-    return [(frame, side) for frame in frames for side in sides]
+    return [(frame, side) for frame in frames for side in (h > 0, h < lax.axis_size("ha") - 1)]
 
 
 def column_masks(pairs, half, pieces):
@@ -114,15 +113,14 @@
 
 
 def keys_values(x_refs, wk_ref, wv_ref, gain_ref, kv_ref):
-    first = 0
-    for x_ref in x_refs:
-        rows = slice(first, first + x_ref.shape[0])
-        first = rows.stop
-        out = jnp.dot(x_ref[...], wk_ref[...], preferred_element_type=f32)
-        for b in range(out.shape[1] // hd):
-            lanes = slice(b * hd, (b + 1) * hd)
-            kv_ref[0, rows, lanes] = normed(out[:, lanes], gain_ref[...])
-        kv_ref[1, rows, :] = jnp.dot(x_ref[...], wv_ref[...], preferred_element_type=f32).astype(bf16)
+    x = jnp.concatenate([ref[...] for ref in x_refs], axis=0)
+    w = jnp.concatenate([wk_ref[...], wv_ref[...]], axis=1)
+    out = jnp.dot(x, w, preferred_element_type=f32)
+    width = wk_ref.shape[1]
+    for b in range(width // hd):
+        lanes = slice(b * hd, (b + 1) * hd)
+        kv_ref[0, :, lanes] = normed(out[:, lanes], gain_ref[...])
+    kv_ref[1] = out[:, width:].astype(bf16)
 
 
 def add_total(s_ref, head, rows, total):
@@ -166,25 +164,23 @@
 
 
 def home_kernel(ext, lens, q_ref, x_ref, wk_ref, wv_ref, gain_ref, o_ref, s_ref, kv_ref, late_ref):
-    step = pl.program_id(0)
     begin(s_ref, None)
     keys_values([x_ref], wk_ref, wv_ref, gain_ref, kv_ref)
     pairs, _ = reach_flags(itself, itself, ext, lens)
     gather(q_ref, None, o_ref, s_ref, [(any_of(pairs), [kv_ref], pairs, home_pieces())])
 
-    @pl.when(step == 0)
+    @pl.when(pl.program_id(0) == 0)
     def _():
         late_ref[...] = x_ref[x_ref.shape[0] // 2 :, :]
 
 
-def first_kernel(ext, lens, xu, xd, wk_ref, wv_ref, gain_ref, near_ref):
+def first_kernel(ext, lens, xu, xd, wk_ref, wv_ref, gain_ref, q_ref, kv_ref, o_ref, s_ref, near_ref):
+    begin(s_ref, None)
+
     @pl.when(near_needed(ext, lens))
     def _():
         keys_values([xu, xd], wk_ref, wv_ref, gain_ref, near_ref)
 
-
-def y_kernel(ext, lens, q_ref, kv_ref, near_ref, o_ref, s_ref):
-    begin(s_ref, None)
     pairs, reach = reach_flags(y_partner, itself, ext, lens)
     active = any_of(pairs)
     gather(
@@ -221,43 +217,52 @@
         o_ref[:, o_ref.shape[1] - hd :] = jnp.where(lane_id() < hd // 2, high, low)
 
 
-def near_kernel(ext, lens, q_ref, a_ref, t_ref, first_ref, last_ref, o_ref, s_ref):
+def own_kernel(ext, lens, q_ref, a_ref, t_ref, n0_ref, n1_ref, core_ref, o_ref, s_ref):
     begin(s_ref, t_ref)
     pairs, reach = reach_flags(itself, itself, ext, lens)
-    keys = [first_ref, last_ref]
-    gather(q_ref, a_ref, o_ref, s_ref, [(any_of(pairs) & reach, keys, pairs, near_pieces([0, 1]))])
-
-
-def core_kernel(ext, lens, q_ref, a_ref, t_ref, home_ref, first_ref, last_ref, o_ref, s_ref):
+    near = near_pieces([0, 1])
+    gather(q_ref, a_ref, o_ref, s_ref, [(any_of(pairs) & reach, [n0_ref, n1_ref], pairs, near)])
+    pairs, _ = reach_flags(itself, core_partner, ext, lens)
+    gather(q_ref, o_ref, o_ref, s_ref, [(any_of(pairs), [core_ref], pairs, home_pieces())])
+
+
+def core_kernel(ext, lens, q_ref, a_ref, t_ref, c0_ref, c1_ref, o_ref, s_ref, part):
     begin(s_ref, t_ref)
     pairs, reach = reach_flags(itself, core_partner, ext, lens)
-    active = any_of(pairs)
-    gather(
-        q_ref,
-        a_ref,
-        o_ref,
-        s_ref,
-        [
-            (active & reach, [home_ref, first_ref, last_ref], pairs, home_pieces() + near_pieces([0, 1])),
-            (active & jnp.logical_not(reach), [home_ref], pairs, home_pieces()),
-        ],
-    )
-
-
-def close_kernel(a_ref, t_ref, y_ref, w_ref, out_ref, mixed):
-    width = a_ref.shape[1]
-    back = y_ref[:, width:].astype(f32)
-    for b in range(width // hd):
+    near = near_pieces([0, 1])
+    gather(q_ref, a_ref, part, s_ref, [(any_of(pairs) & reach, [c0_ref, c1_ref], pairs, near)])
+    o_ref[...] = part[...].astype(bf16)
+
+
+def close_kernel(a_ref, t_ref, y_ref, back_ref, w_ref, out_ref, total):
+    step = pl.program_id(0)
+    count = a_ref.shape[1] // hd
+    low = back_ref[...].astype(f32)
+    sums = t_ref[...] + (low + pltpu.roll(low, hd // 2, 1))
+    values = []
+    for b in range(count):
         lanes = slice(b * hd, (b + 1) * hd)
-        low = hd // 2 + b
-        total = t_ref[:, b : b + 1] + (back[:, b : b + 1] + back[:, low : low + 1])
-        value = a_ref[:, lanes] + y_ref[:, lanes].astype(f32)
-        mixed[:, lanes] = (value / total).astype(bf16)
-    out_ref[...] = jnp.dot(mixed[...], w_ref[...], preferred_element_type=f32).astype(bf16)
+        sum_b = jnp.sum(jnp.where(lane_id() == step * count + b, sums, 0.0), axis=1, keepdims=True)
+        value = a_ref[:, lanes].astype(f32) + y_ref[:, lanes].astype(f32)
+        values.append((value / sum_b).astype(bf16))
+    mixed = values[0] if count == 1 else jnp.concatenate(values, axis=1)
+    part = jnp.dot(mixed, w_ref[...], preferred_element_type=f32)
+
+    @pl.when(step == 0)
+    def _():
+        total[...] = part
+
+    @pl.when((step > 0) & (step < pl.num_programs(0) - 1))
+    def _():
+        total[...] += part
+
+    @pl.when(step == pl.num_programs(0) - 1)
+    def _():
+        out_ref[...] = (total[...] + part).astype(bf16)
 
 
 def whole(shape):
-    return pl.BlockSpec(shape, lambda g: (0,) * len(shape))
+    return pl.BlockSpec(shape, lambda g: (0,) * len(shape), pipeline_mode=pl.Buffered(1))
 
 
 def by_group(rows):
@@ -321,6 +326,9 @@
     flags = [(extents, smem), (clip_lengths, smem)]
     kv_weights = [w_of(1), w_of(2), (k_gain, whole((1, hd)))]
 
+    def partial(acc, total):
+        return [(acc, by_group(tile)), (total, total_spec)]
+
     up_first, down_first = to_heights(activations[0].reshape(half, model))
     (q,) = call(
         project_kernel,
@@ -340,28 +348,18 @@
     up_last, down_last = to_heights(late)
     kv_core = to_core(kv_home)
 
-    def partial(acc, total):
-        return [(acc, by_group(tile)), (total, total_spec)]
-
     def neighbours(up, down):
         return [(up, whole((half, model))), (down, whole((half, model)))]
 
-    (near_first,) = call(
+    y, y_total, near_first = call(
         first_kernel,
         steps,
-        flags + neighbours(up_first, down_first) + kv_weights,
-        [kv_out],
-        2 * mat,
+        flags + neighbours(up_first, down_first) + kv_weights + [(q_y, by_group(tile)), (kv_home, kv_spec)],
+        sums + [kv_out],
+        2 * unit + 2 * mat,
         after=own_total,
     )
     near_first_core = to_core(near_first)
-    y, y_total = call(
-        y_kernel,
-        steps,
-        flags + [(q_y, by_group(tile)), (kv_home, kv_spec), (near_first, kv_spec)],
-        sums,
-        2 * unit,
-    )
     wide = (tile, inner + hd)
     y_part, near_last = call(
         second_kernel,
@@ -373,33 +371,42 @@
     )
     y_back = to_y(y_part)
     near_last_core = to_core(near_last)
-
     own, own_total = call(
-        near_kernel,
-        steps,
-        flags + [(q, by_group(tile))] + partial(own, own_total) + [(near_first, kv_spec), (near_last, kv_spec)],
-        sums,
-        2 * unit,
-    )
-    own, own_total = call(
-        core_kernel,
+        own_kernel,
         steps,
         flags
         + [(q, by_group(tile))]
         + partial(own, own_total)
-        + [(kv, kv_spec) for kv in (kv_core, near_first_core, near_last_core)],
+        + [(kv, kv_spec) for kv in (near_first, near_last, kv_core)],
         sums,
         3 * unit,
     )
-    cut = tile // 4
+    own, own_total = call(
+        core_kernel,
+        steps,
+        flags
+        + [(q, by_group(tile))]
+        + partial(own, own_total)
+        + [(kv, kv_spec) for kv in (near_first_core, near_last_core)],
+        [(by_group(tile), (tile, inner), bf16), sums[1]],
+        2 * unit,
+        [pltpu.VMEM((tile, group * hd), f32)],
+    )
+    heads = 2
+    close_spec = pl.BlockSpec((tile, heads * hd), lambda g: (0, g))
     (result,) = call(
         close_kernel,
-        4,
-        [(a, pl.BlockSpec((cut, a.shape[1]), lambda g: (g, 0))) for a in (own, own_total, y_back)]
-        + [(out_weight, whole((inner, model)))],
-        [(pl.BlockSpec((cut, model), lambda g: (g, 0)), (tile, model), bf16)],
+        inner // (heads * hd),
+        [
+            (own, close_spec),
+            (own_total, total_spec),
+            (y_back, close_spec),
+            (y_back, pl.BlockSpec((tile, hd), lambda g: (0, inner // hd))),
+            (out_weight, pl.BlockSpec((heads * hd, model), lambda g: (g, 0))),
+        ],
+        [(whole((tile, model)), (tile, model), bf16)],
         mat,
-        [pltpu.VMEM((cut, inner), bf16)],
+        [pltpu.VMEM((tile, model), f32)],
     )
     return result.reshape(frames, rows, cols, model)
 

time: 145 us -> 168 us (1.16)
  the two profiles are of different devices: /device:TPU:49 before, /device:TPU:14 now
where the time goes in v1:
time: 168 us; the launch traced here: 165 us
  Pallas kernels  120 us (71%)
  starting transfers between devices  42.3 us (25%)
  waiting for transfers between devices  1.81 us (1%)
    pallas_call x7, Pallas kernels, call(): pl.pallas_call(run, grid=(steps,), in_specs=specs, out_specs=[spec for sp...  120 us
    ppermute x2, starting transfers between devices, to_y(): return lax.ppermute(a, 'ta', route + [(b, a) for a, b in route])  24.6 us
    ppermute x2, starting transfers between devices, to_heights(): lax.ppermute(a, 'ha', [(i + 1, i) for i in range(height - 1)])  12.2 us
    ppermute x2, starting transfers between devices, to_heights(): lax.ppermute(a, 'ha', [(i, i + 1) for i in range(height - 1)])  3.84 us
  transfers between devices with their start and end apart: 9, of which 1 were waited for; matrix products, arithmetic and copies ran while one was open for 0% of the time, Pallas kernels for 60%

profile of v1, /device:TPU:14, one launch (start us, length us, event | category | flops | bytes accessed | tf_op | source)
XLA Modules:
  0.0 165.5 jit_solution(10422981402166642781)
XLA Ops:
  0.0 0.0 copy-start
  0.0 0.0 copy-start.1
  0.0 7.6 %shard_map.73.q_ref = bf16[640,1536]{1,0:T(8,128)(2,1)} custom-call(bf16[640,1536]{1,0:T(8,128)(2,1)} %bitcast.7, bf16[1536,4608]{1,0:T(8,128)(2,1)} %wv_ref.3, f32[1,128]{1,0:T(1,128)} %bitcast.9), custom_call_target="tpu_custom_call" | custom-call | flops 7549747200 | bytes 1 | tf_op jit(solution)/shard_map/pallas_call | solution.py:281
  7.6 1.9 %collective-permute-start.2 = (bf16[640,1536]{1,0:T(8,128)(2,1)}, bf16[640,1536]{1,0:T(8,128)(2,1)}, u32[]{:S(2)}, u32[]{:S(2)}) collective-permute-start(bf16[640,1536]{1,0:T(8,128)(2,1)} %shard_map.73.q_ref), channel_id=1, source_target_pairs={{8,16},{24,32},{40,48},{56,64},{72,80},{88,96},{104,112},{16,8},{3... | collective-permute-start | bytes 5898248 | tf_op jit(solution)/shard_map/ppermute | solution.py:315
  9.5 0.0 copy-done
  9.5 0.1 slice.3
  9.6 6.2 %collective-permute-start.1 = (bf16[320,1536]{1,0:T(8,128)(2,1)S(1)}, bf16[320,1536]{1,0:T(8,128)(2,1)S(1)}, u32[]{:S(2)}, u32[]{:S(2)}) collective-permute-start(bf16[320,1536]{1,0:T(8,128)(2,1)S(1)} %bitcast.5), channel_id=1, source_target_pairs={{1,0},{2,1},{3,2},{4,3},{5,4},{6,5},{7,6},{9,8},{10,9},{11,10},{12... | collective-permute-start | bytes 2949128 | tf_op jit(solution)/shard_map/ppermute | solution.py:307
  15.8 1.9 %collective-permute-start = (bf16[320,1536]{1,0:T(8,128)(2,1)S(1)}, bf16[320,1536]{1,0:T(8,128)(2,1)}, u32[]{:S(2)}, u32[]{:S(2)}) collective-permute-start(bf16[320,1536]{1,0:T(8,128)(2,1)S(1)} %bitcast.6), channel_id=1, source_target_pairs={{0,1},{1,2},{2,3},{3,4},{4,5},{5,6},{6,7},{8,9},{9,10},{10,11},{11... | collective-permute-start | bytes 2949128 | tf_op jit(solution)/shard_map/ppermute | solution.py:306
  17.7 0.0 copy-done.1
  17.7 0.7 copy.12.ext.refs_0_
  18.5 18.3 %shard_map.74 = (f32[640,1536]{1,0:T(8,128)}, f32[640,128]{1,0:T(8,128)}, bf16[2,640,1536]{2,1,0:T(8,128)(2,1)}, bf16[320,1536]{1,0:T(8,128)(2,1)}) custom-call(s32[16,8,2]{2,1,0:T(8,128)} %copy.12.ext.refs_0_, s32[4]{0:T(128)} %lens.7, bf16[640,1536]{1,0:T(8,128)(2,1)} %shard_map.73.q_ref, bf16[640,1536]{1,0:T(8,128)(2,1)} %bitcast.8, ...), custom_call_target="tpu_custom_call" | custom-call | flops 18245222400 | bytes 1 | tf_op jit(solution)/shard_map/pallas_call | solution.py:281
  36.8 6.0 %collective-permute-start.4 = (bf16[320,1536]{1,0:T(8,128)(2,1)}, bf16[320,1536]{1,0:T(8,128)(2,1)S(1)}, u32[]{:S(2)}, u32[]{:S(2)}) collective-permute-start(bf16[320,1536]{1,0:T(8,128)(2,1)} %get-tuple-element.22), channel_id=1, source_target_pairs={{1,0},{2,1},{3,2},{4,3},{5,4},{6,5},{7,6},{9,8},{10,9},{11,10},{12... | collective-permute-start | bytes 2949128 | tf_op jit(solution)/shard_map/ppermute | solution.py:307
  42.8 1.9 %collective-permute-start.3 = (bf16[320,1536]{1,0:T(8,128)(2,1)}, bf16[320,1536]{1,0:T(8,128)(2,1)}, u32[]{:S(2)}, u32[]{:S(2)}) collective-permute-start(bf16[320,1536]{1,0:T(8,128)(2,1)} %get-tuple-element.22), channel_id=1, source_target_pairs={{0,1},{1,2},{2,3},{3,4},{4,5},{5,6},{6,7},{8,9},{9,10},{10,11},{11... | collective-permute-start | bytes 2949128 | tf_op jit(solution)/shard_map/ppermute | solution.py:306
  44.7 0.0 collective-permute-done.1.refs_3_
  44.7 0.0 copy-start.3
  44.7 1.1 collective-permute-start.5
  45.8 0.0 collective-permute-done.refs_2_
  45.8 0.0 collective-permute-done.2.refs_7_.q_ref
  45.8 0.0 copy-done.3
  45.9 23.9 %shard_map.75 = (f32[640,1536]{1,0:T(8,128)}, f32[640,128]{1,0:T(8,128)}, bf16[2,640,1536]{2,1,0:T(8,128)(2,1)}) custom-call(s32[16,8,2]{2,1,0:T(8,128)} %copy.12.ext.refs_0_, s32[4]{0:T(128)} %lens.7, bf16[320,1536]{1,0:T(8,128)(2,1)} %collective-permute-done.refs_2_, bf16[320,1536]{1,0:T(8,128)(2,1)} %copy-done.3, bf16[1536,4608]{1,0:T(8,128)(2,1)} %wv_ref.3, ...), custom_call_target="tpu_custom_call" | custom-call | flops 21390950400 | bytes 1 | tf_op jit(solution)/shard_map/pallas_call | solution.py:281
  69.8 0.0 collective-permute-done.4.xd
  69.8 0.0 copy-start.4
  69.8 1.8 %collective-permute-done.3.xu = bf16[320,1536]{1,0:T(8,128)(2,1)} collective-permute-done((bf16[320,1536]{1,0:T(8,128)(2,1)}, bf16[320,1536]{1,0:T(8,128)(2,1)}, u32[]{:S(2)}, u32[]{:S(2)}) %collective-permute-start.3) | collective-permute-done | bytes 983072 | tf_op jit(solution)/shard_map/ppermute | solution.py:306
  71.6 0.0 copy-done.4
  71.6 0.0 copy-start.2
  71.6 19.7 %shard_map.76 = (bf16[640,1664]{1,0:T(8,128)(2,1)}, bf16[2,640,1536]{2,1,0:T(8,128)(2,1)}) custom-call(s32[16,8,2]{2,1,0:T(8,128)} %copy.12.ext.refs_0_, s32[4]{0:T(128)} %lens.7, bf16[320,1536]{1,0:T(8,128)(2,1)} %collective-permute-done.3.xu, bf16[320,1536]{1,0:T(8,128)(2,1)} %copy-done.4, bf16[1536,4608]{1,0:T(8,128)(2,1)} %wv_ref.3, ...), custom_call_target="tpu_custom_call" | custom-call | flops 18245222400 | bytes 1 | tf_op jit(solution)/shard_map/pallas_call | solution.py:281
  91.3 0.0 collective-permute-start.7
  91.3 0.0 copy-done.2
  91.3 0.5 collective-permute-start.6
  91.8 22.7 %collective-permute-start.8 = (bf16[640,1664]{1,0:T(8,128)(2,1)}, bf16[640,1664]{1,0:T(8,128)(2,1)}, u32[]{:S(2)}, u32[]{:S(2)}) collective-permute-start(bf16[640,1664]{1,0:T(8,128)(2,1)} %get-tuple-element.30), channel_id=1, source_target_pairs={{8,16},{24,32},{40,48},{56,64},{72,80},{88,96},{104,112},{16,8},{3... | collective-permute-start | bytes 6389768 | tf_op jit(solution)/shard_map/ppermute | solution.py:315
  114.5 0.0 collective-permute-done.5.core_ref
  114.5 22.5 %shard_map.77 = (f32[640,1536]{1,0:T(8,128)}, f32[640,128]{1,0:T(8,128)}) custom-call(s32[16,8,2]{2,1,0:T(8,128)} %copy.12.ext.refs_0_, s32[4]{0:T(128)} %lens.7, bf16[640,1536]{1,0:T(8,128)(2,1)} %shard_map.73.q_ref, f32[640,1536]{1,0:T(8,128)} %get-tuple-element.18.a_ref, f32[640,128]{1,0:T(8,128)} %get-tuple-element.19.refs_9_.t_ref, ...), custom_call_target="tpu_custom_call" | custom-call | flops 9437184000 | bytes 1 | tf_op jit(solution)/shard_map/pallas_call | solution.py:281
  137.0 0.0 collective-permute-done.7.c1_ref
  137.0 0.0 collective-permute-done.6.c0_ref
  137.1 15.5 %shard_map.78 = (bf16[640,1536]{1,0:T(8,128)(2,1)}, f32[640,128]{1,0:T(8,128)}) custom-call(s32[16,8,2]{2,1,0:T(8,128)} %copy.12.ext.refs_0_, s32[4]{0:T(128)} %lens.7, bf16[640,1536]{1,0:T(8,128)(2,1)} %shard_map.73.q_ref, f32[640,1536]{1,0:T(8,128)} %get-tuple-element.26.a_ref, f32[640,128]{1,0:T(8,128)} %get-tuple-element.27.t_ref, ...), custom_call_target="tpu_custom_call" | custom-call | flops 6291456000 | bytes 1 | tf_op jit(solution)/shard_map/pallas_call | solution.py:281
  152.6 0.0 collective-permute-done.8.y_ref.back_ref
  152.6 12.9 %shard_map.79 = bf16[640,1536]{1,0:T(8,128)(2,1)} custom-call(bf16[640,1536]{1,0:T(8,128)(2,1)} %get-tuple-element.28.a_ref, f32[640,128]{1,0:T(8,128)} %get-tuple-element.29.t_ref, bf16[640,1664]{1,0:T(8,128)(2,1)} %collective-permute-done.8.y_ref.back_ref, bf16[640,1664]{1,0:T(8,128)(2,1)} %collective-permute-done.8.y_ref.back_ref, bf16[1536,1536]{1,0:T(8,128)(2,1)} %w_ref.3), custom_call_target="tpu_custom_call" | custom-call | flops 7549747200 | bytes 1 | tf_op jit(solution)/shard_map/pallas_call | solution.py:281
Async XLA Ops:
  0.0 9.5 %copy-start = (bf16[2,4,80,1536]{3,2,1,0:T(8,128)(2,1)S(1)}, bf16[2,4,80,1536]{3,2,1,0:T(8,128)(2,1)}, u32[]{:S(2)}) copy-start(bf16[2,4,80,1536]{3,2,1,0:T(8,128)(2,1)} %param.7) | copy-start | bytes 5898244
  0.0 17.7 %copy-start.1 = (s32[16,8,2]{0,2,1:T(2,128)S(1)}, s32[16,8,2]{0,2,1:T(2,128)}, u32[]{:S(2)}) copy-start(s32[16,8,2]{0,2,1:T(2,128)} %param.13) | copy-start | bytes 3076
  7.6 38.3 %collective-permute-start.2 = (bf16[640,1536]{1,0:T(8,128)(2,1)}, bf16[640,1536]{1,0:T(8,128)(2,1)}, u32[]{:S(2)}, u32[]{:S(2)}) collective-permute-start(bf16[640,1536]{1,0:T(8,128)(2,1)} %shard_map.73.q_ref), channel_id=1, source_target_pairs={{8,16},{24,32},{40,48},{56,64},{72,80},{88,96},{104,112},{16,8},{3... | collective-permute-start | bytes 5898248 | tf_op jit(solution)/shard_map/ppermute | solution.py:315
  9.6 35.2 %collective-permute-start.1 = (bf16[320,1536]{1,0:T(8,128)(2,1)S(1)}, bf16[320,1536]{1,0:T(8,128)(2,1)S(1)}, u32[]{:S(2)}, u32[]{:S(2)}) collective-permute-start(bf16[320,1536]{1,0:T(8,128)(2,1)S(1)} %bitcast.5), channel_id=1, source_target_pairs={{1,0},{2,1},{3,2},{4,3},{5,4},{6,5},{7,6},{9,8},{10,9},{11,10},{12... | collective-permute-start | bytes 2949128 | tf_op jit(solution)/shard_map/ppermute | solution.py:307
  15.8 30.1 %collective-permute-start = (bf16[320,1536]{1,0:T(8,128)(2,1)S(1)}, bf16[320,1536]{1,0:T(8,128)(2,1)}, u32[]{:S(2)}, u32[]{:S(2)}) collective-permute-start(bf16[320,1536]{1,0:T(8,128)(2,1)S(1)} %bitcast.6), channel_id=1, source_target_pairs={{0,1},{1,2},{2,3},{3,4},{4,5},{5,6},{6,7},{8,9},{9,10},{10,11},{11... | collective-permute-start | bytes 2949128 | tf_op jit(solution)/shard_map/ppermute | solution.py:306
  36.8 33.1 %collective-permute-start.4 = (bf16[320,1536]{1,0:T(8,128)(2,1)}, bf16[320,1536]{1,0:T(8,128)(2,1)S(1)}, u32[]{:S(2)}, u32[]{:S(2)}) collective-permute-start(bf16[320,1536]{1,0:T(8,128)(2,1)} %get-tuple-element.22), channel_id=1, source_target_pairs={{1,0},{2,1},{3,2},{4,3},{5,4},{6,5},{7,6},{9,8},{10,9},{11,10},{12... | collective-permute-start | bytes 2949128 | tf_op jit(solution)/shard_map/ppermute | solution.py:307
  42.8 28.8 %collective-permute-start.3 = (bf16[320,1536]{1,0:T(8,128)(2,1)}, bf16[320,1536]{1,0:T(8,128)(2,1)}, u32[]{:S(2)}, u32[]{:S(2)}) collective-permute-start(bf16[320,1536]{1,0:T(8,128)(2,1)} %get-tuple-element.22), channel_id=1, source_target_pairs={{0,1},{1,2},{2,3},{3,4},{4,5},{5,6},{6,7},{8,9},{9,10},{10,11},{11... | collective-permute-start | bytes 2949128 | tf_op jit(solution)/shard_map/ppermute | solution.py:306
  44.7 1.1 copy-start.3
  44.7 69.8 %collective-permute-start.5 = (bf16[2,640,1536]{2,1,0:T(8,128)(2,1)}, bf16[2,640,1536]{2,1,0:T(8,128)(2,1)}, u32[]{:S(2)}, u32[]{:S(2)}) collective-permute-start(bf16[2,640,1536]{2,1,0:T(8,128)(2,1)} %get-tuple-element.20.refs_8_), channel_id=1, source_target_pairs={{0,8},{8,0},{16,24},{24,16},{32,40},{40,32},{48,56},{56,48},{64,72... | collective-permute-start | bytes 11796488 | tf_op jit(solution)/shard_map/ppermute | solution.py:311
  69.8 1.8 %copy-start.4 = (bf16[320,1536]{1,0:T(8,128)(2,1)}, bf16[320,1536]{1,0:T(8,128)(2,1)S(1)}, u32[]{:S(2)}) copy-start(bf16[320,1536]{1,0:T(8,128)(2,1)S(1)} %collective-permute-done.4.xd) | copy-start | bytes 2949124
  71.6 19.7 %copy-start.2 = (bf16[2,640,1536]{2,1,0:T(8,128)(2,1)S(1)}, bf16[2,640,1536]{2,1,0:T(8,128)(2,1)}, u32[]{:S(2)}) copy-start(bf16[2,640,1536]{2,1,0:T(8,128)(2,1)} %get-tuple-element.21.n0_ref) | copy-start | bytes 11796484
  91.3 45.8 %collective-permute-start.7 = (bf16[2,640,1536]{2,1,0:T(8,128)(2,1)}, bf16[2,640,1536]{2,1,0:T(8,128)(2,1)}, u32[]{:S(2)}, u32[]{:S(2)}) collective-permute-start(bf16[2,640,1536]{2,1,0:T(8,128)(2,1)} %get-tuple-element.25.n1_ref), channel_id=1, source_target_pairs={{0,8},{8,0},{16,24},{24,16},{32,40},{40,32},{48,56},{56,48},{64,72... | collective-permute-start | bytes 11796488 | tf_op jit(solution)/shard_map/ppermute | solution.py:311
  91.3 45.7 %collective-permute-start.6 = (bf16[2,640,1536]{2,1,0:T(8,128)(2,1)S(1)}, bf16[2,640,1536]{2,1,0:T(8,128)(2,1)}, u32[]{:S(2)}, u32[]{:S(2)}) collective-permute-start(bf16[2,640,1536]{2,1,0:T(8,128)(2,1)S(1)} %copy-done.2), channel_id=1, source_target_pairs={{0,8},{8,0},{16,24},{24,16},{32,40},{40,32},{48,56},{56,48},{64,72... | collective-permute-start | bytes 11796488 | tf_op jit(solution)/shard_map/ppermute | solution.py:311
  91.8 60.8 %collective-permute-start.8 = (bf16[640,1664]{1,0:T(8,128)(2,1)}, bf16[640,1664]{1,0:T(8,128)(2,1)}, u32[]{:S(2)}, u32[]{:S(2)}) collective-permute-start(bf16[640,1664]{1,0:T(8,128)(2,1)} %get-tuple-element.30), channel_id=1, source_target_pairs={{8,16},{24,32},{40,48},{56,64},{72,80},{88,96},{104,112},{16,8},{3... | collective-permute-start | bytes 6389768 | tf_op jit(solution)/shard_map/ppermute | solution.py:315
